TPU v7x, 32 devices: a whole 2x2x4 slice. The times are simulated.
32 devices in a mesh: groups: 2 (over y), expert: 16 (over z, x, core), tensor: 1.
Axes of the slice: x: 2, y: 2, z: 4, core: 2. Of those that a mesh axis runs over, the one named last changes fastest.
Arguments:
- attn_part: bfloat16 [1, 2048, 3584], P('tensor', ('groups', 'expert')), parts along dimension 1, may hold values from -64 to 64
- resid: bfloat16 [2048, 3584], P(('groups', 'expert')), parts along dimension 0, may hold values from -6 to 6
- norm_gain: bfloat16 [3584], replicated, may hold values from 0.25 to 1.75
- routes: int32 [2048, 8], P(('groups', 'expert')), parts along dimension 0, may hold values from 0 to 15, all different within a row; in each aligned block of 64 rows (0 to 63, 64 to 127, ...) at most 64 rows name the same one
- gate_codes: int32 [2048, 8], P(('groups', 'expert')), parts along dimension 0, may hold values from 1 to 4095
- w_gate: bfloat16 [16, 3584, 1024], P('expert', None, 'tensor'), may hold values from -0.09375 to 0.09375
- w_up: bfloat16 [16, 3584, 1024], P('expert', None, 'tensor'), may hold values from -0.09375 to 0.09375
- w_down: bfloat16 [16, 1024, 3584], P('expert', 'tensor'), may hold values from -0.1875 to 0.1875
Outputs:
- moe_out: bfloat16 [2048, 3584], P(('groups', 'expert'), 'tensor'), parts along dimension 0
There are 2 independent parts, one for each index of `groups`. A program takes and returns all parts, laid end to end along the dimension named above; an argument that names none is the same for every part. Nothing has to cross between parts.
Inputs may be any that keep to these rules, and one draw needn't show every extreme that they name: `routes`: each row names 8 different experts; among the rows of one device no expert is named by more than 64 rows, a bound that some block reaches.
All inputs are finite; a program needn't handle non-finite values.
Results may differ from a plain program's by a relative error of at most 0.035.
Values may be sent and summed in bfloat16 or wider, within the bound.
A program may use at most 192 MiB of HBM per device.

v0:
```python
import jax
import jax.numpy as jnp
from jax import lax
from jax.sharding import PartitionSpec as P


def expert_output(hidden, w_down):
    partial_out = jnp.einsum("sekf,efd->sekd", hidden, w_down, preferred_element_type=jnp.float32)
    return lax.all_to_all(
        partial_out.astype(jnp.bfloat16), "expert", split_axis=0, concat_axis=0, tiled=True
    )


def per_device(attn_part, resid, norm_gain, routes, gate_codes, w_gate, w_up, w_down):
    tok_count = routes.shape[0]
    top_count = routes.shape[1]
    n_expert = lax.axis_size("expert")
    local_experts = w_gate.shape[0]
    experts_all = n_expert * local_experts
    capacity = min(tok_count, 3 * tok_count * top_count // experts_all)
    flat_routes = routes.reshape(-1)
    onehot = (flat_routes[:, None] == jnp.arange(experts_all, dtype=jnp.int32)[None, :]).astype(
        jnp.int32
    )
    ranks = jnp.cumsum(onehot, axis=0) - onehot
    slot_of = jnp.sum(ranks * onehot, axis=1)
    target = flat_routes * capacity + slot_of
    tok_index = jnp.arange(tok_count * top_count, dtype=jnp.int32) // top_count
    codes = gate_codes.astype(jnp.float32)
    weights = (codes / jnp.sum(codes, axis=1, keepdims=True)).reshape(-1)
    head_total = lax.psum(attn_part[0].astype(jnp.float32).astype(jnp.bfloat16), "tensor").astype(
        jnp.float32
    )
    stream = resid.astype(jnp.float32) + head_total
    mean_sq = jnp.mean(stream * stream, axis=1, keepdims=True)
    normed = (stream * lax.rsqrt(mean_sq + 1e-06) * norm_gain.astype(jnp.float32)).astype(
        jnp.bfloat16
    )
    cols = normed.shape[1]
    buffer = jnp.zeros((experts_all * capacity, cols), jnp.bfloat16)
    buffer = buffer.at[target].set(normed[tok_index])
    outgoing = buffer.reshape(n_expert, local_experts, capacity, cols)
    received = lax.all_to_all(outgoing, "expert", split_axis=0, concat_axis=0, tiled=True)
    gate = jnp.einsum("sekd,edf->sekf", received, w_gate, preferred_element_type=jnp.float32)
    up = jnp.einsum("sekd,edf->sekf", received, w_up, preferred_element_type=jnp.float32)
    hidden = (jax.nn.silu(gate) * up).astype(jnp.bfloat16)
    returned = expert_output(hidden, w_down)
    out_cols = returned.shape[3]
    picked = returned.reshape(experts_all * capacity, out_cols)[target]
    weighted = picked.astype(jnp.float32) * weights[:, None]
    combined = jnp.sum(weighted.reshape(tok_count, top_count, out_cols), axis=1)
    return lax.psum_scatter(
        combined.astype(jnp.bfloat16), "tensor", scatter_dimension=1, tiled=True
    )


def solution(mesh):
    return jax.shard_map(
        per_device,
        mesh=mesh,
        in_specs=(
            P("tensor", ("groups", "expert"), None),
            P(("groups", "expert"), None),
            P(),
            P(("groups", "expert"), None),
            P(("groups", "expert"), None),
            P("expert", None, "tensor"),
            P("expert", None, "tensor"),
            P("expert", "tensor", None),
        ),
        out_specs=P(("groups", "expert"), "tensor"),
        check_vma=False,
    )
```

profile of v0, /device:TPU:15, one launch (start us, length us, event | category | flops | bytes accessed | tf_op | source)
XLA Modules:
  0.0 406.1 jit_solution(17923692108606832274)
XLA Ops:
  0.0 0.8 copy.16
  0.8 0.1 eq.29
  0.9 0.1 eq.25
  1.0 0.7 broadcast_multiply_fusion
  1.7 1.2 reduce-window.6
  2.8 0.2 slice_reduce_fusion
  3.1 0.1 copy.15
  3.2 0.1 mul.52
  3.3 0.7 convert_element_type.57
  4.0 1.4 multiply_reduce_fusion
  5.4 0.1 fusion.25
  5.5 1.3 multiply_convert_fusion
  6.8 20.7 %scatter_custom_fusion = bf16[1024,3584]{1,0:T(8,128)(2,1)} fusion(s32[512]{0:T(512)S(1)} %bitcast.91, bf16[64,3584]{1,0:T(8,128)(2,1)S(1)} %multiply_convert_fusion, s32[1024]{0:T(1024)S(1)} %pad_clamp_fusion.1, bf16[]{:T(256)} %constant.28.clone.1), kind=kCustom, calls=%fused_computation.21 | custom fusion | bytes 7340034 | tf_op jit(solution)/shard_map/scatter | solution.py:41
  27.6 0.0 slice-start
  27.6 166.5 %all_to_all.10 = bf16[16,1,64,3584]{3,2,1,0:T(8,128)(2,1)S(1)} all-to-all(bf16[16,1,64,3584]{3,2,1,0:T(8,128)(2,1)} %bitcast.90), channel_id=1, replica_groups=mesh['groups'=2,'expert'=16,'tensor'=1] {'expert'}, dimensions={0} | all-to-all | bytes 14680064 | tf_op jit(solution)/shard_map/all_to_all | solution.py:43
  194.0 0.0 slice-start.1
  194.0 0.0 slice-start.2
  194.0 10.1 %fusion.2 = f32[16,64,1024]{2,1,0:T(8,128)S(1)} fusion(bf16[1,3584,1024]{2,1,0:T(8,128)(2,1)} %param.14, bf16[16,1,64,3584]{3,2,1,0:T(8,128)(2,1)S(1)} %all_to_all.10), kind=kOutput, calls=%fused_computation.7 | convolution fusion | flops 7516192768 | bytes 18874368 | tf_op jit(solution)/shard_map/sekd,edf->sekf/dot_general | solution.py:45
  204.1 0.0 slice-done
  204.1 0.0 slice-done.1
  204.2 0.0 slice-start.3
  204.2 8.6 %fusion.11 = bf16[16,1,64,1024]{3,2,0,1:T(8,128)(2,1)S(1)} fusion(f32[16,64,1024]{2,1,0:T(8,128)S(1)} %fusion.2, bf16[1,3584,1024]{2,1,0:T(8,128)(2,1)S(1)} %bitcast.96, bf16[16,1,64,3584]{3,2,1,0:T(8,128)(2,1)S(1)} %all_to_all.10), kind=kOutput, calls=%fused_computation.15 | convolution fusion | flops 7522484224 | bytes 20971520 | tf_op jit(solution)/shard_map/sekd,edf->sekf/dot_general | solution.py:44
  212.8 0.0 slice-done.2
  212.8 0.0 slice-done.3
  212.8 9.9 %fusion.8 = bf16[16,1,64,3584]{3,2,1,0:T(8,128)(2,1)} fusion(bf16[1,1024,3584]{2,1,0:T(8,128)(2,1)S(1)} %bitcast.98, bf16[16,1,64,1024]{3,2,0,1:T(8,128)(2,1)S(1)} %fusion.11), kind=kOutput, calls=%fused_computation.13 | convolution fusion | flops 7519862784 | bytes 16777216 | tf_op jit(solution)/shard_map/sekf,efd->sekd/dot_general | solution.py:8
  222.7 0.0 copy-start
  222.7 5.8 %all-to-all-start.1 = ((bf16[16,1,64,3584]{3,2,1,0:T(8,128)(2,1)}), bf16[16,1,64,3584]{3,2,1,0:T(8,128)(2,1)}, u32[]{:S(2)}, u32[]{:S(2)}) async-start(bf16[16,1,64,3584]{3,2,1,0:T(8,128)(2,1)} %fusion.8), calls=%async_computation.1 | async-start | bytes 14680064 | tf_op jit(solution)/shard_map/all_to_all | solution.py:9
  228.4 0.0 copy-done
  228.5 0.1 copy.20
  228.6 159.7 %all-to-all-done.1 = bf16[16,1,64,3584]{3,2,1,0:T(8,128)(2,1)} async-done(((bf16[16,1,64,3584]{3,2,1,0:T(8,128)(2,1)}), bf16[16,1,64,3584]{3,2,1,0:T(8,128)(2,1)}, u32[]{:S(2)}, u32[]{:S(2)}) %all-to-all-start.1) | async-done | bytes 7340064 | tf_op jit(solution)/shard_map/all_to_all | solution.py:9
  388.3 11.9 %gather_fusion = bf16[512,3584]{1,0:T(8,128)(2,1)} fusion(bf16[1024,3584]{1,0:T(8,128)(2,1)} %bitcast.26, s32[1024]{0:T(1024)S(1)} %pad_clamp_fusion), kind=kCustom, calls=%fused_computation.1 | custom fusion | bytes 7342080 | tf_op jit(solution)/shard_map/gather | solution.py:49
  400.2 5.8 %fusion = bf16[64,3584]{1,0:T(8,128)(2,1)} fusion(bf16[512,3584]{1,0:T(8,128)(2,1)} %gather_fusion, f32[64,8]{1,0:T(8,128)S(1)} %copy.20), kind=kLoop, calls=%fused_computation.5 | loop fusion | flops 5275648 | bytes 4130816 | tf_op jit(solution)/shard_map/reduce_sum | solution.py:51
  (12 shorter events, 0.1 us)
Async XLA Ops:
  27.6 176.6 %slice-start = ((s8[7340032]{0:T(1024)(128)(4,1)}), s8[4194304]{0:T(1024)(128)(4,1)S(1)}, s32[]{:S(2)}) async-start(s8[7340032]{0:T(1024)(128)(4,1)} %bitcast.95), calls=%async_computation.2 | async-start | bytes 8388608
  194.0 10.1 %slice-start.1 = ((s8[7340032]{0:T(1024)(128)(4,1)}), s8[3145728]{0:T(1024)(128)(4,1)S(1)}, s32[]{:S(2)}) async-start(s8[7340032]{0:T(1024)(128)(4,1)} %bitcast.95), calls=%async_computation.3 | async-start | bytes 6291456
  194.0 18.7 %slice-start.2 = ((s8[7340032]{0:T(1024)(128)(4,1)}), s8[4194304]{0:T(1024)(128)(4,1)S(1)}, s32[]{:S(2)}) async-start(s8[7340032]{0:T(1024)(128)(4,1)} %bitcast.97), calls=%async_computation.4 | async-start | bytes 8388608
  204.2 8.6 %slice-start.3 = ((s8[7340032]{0:T(1024)(128)(4,1)}), s8[3145728]{0:T(1024)(128)(4,1)S(1)}, s32[]{:S(2)}) async-start(s8[7340032]{0:T(1024)(128)(4,1)} %bitcast.97), calls=%async_computation.5 | async-start | bytes 6291456
  222.7 5.8 %copy-start = (s32[64,8]{0,1:T(8,128)S(1)}, s32[64,8]{0,1:T(8,128)}, u32[]{:S(2)}) copy-start(s32[64,8]{0,1:T(8,128)} %param.12) | copy-start | bytes 6148
  222.7 165.6 %all-to-all-start.1 = ((bf16[16,1,64,3584]{3,2,1,0:T(8,128)(2,1)}), bf16[16,1,64,3584]{3,2,1,0:T(8,128)(2,1)}, u32[]{:S(2)}, u32[]{:S(2)}) async-start(bf16[16,1,64,3584]{3,2,1,0:T(8,128)(2,1)} %fusion.8), calls=%async_computation.1 | async-start | bytes 14680064 | tf_op jit(solution)/shard_map/all_to_all | solution.py:9
where the time goes:
time: 407 us; the launch traced here: 406 us
  blocking collectives  166 us (41%)
  waiting for transfers between devices  160 us (39%)
  local copies, waits for them, and re-layouts  34.1 us (8%)
  matrix products  28.5 us (7%)
  other arithmetic  11.3 us (3%)
  starting transfers between devices  5.76 us (1%)
    all_to_all x1, blocking collectives, per_device(): lax.all_to_all(outgoing, 'expert', split_axis=0, concat_axis=0, tiled=True)  166 us
    all_to_all x1, waiting for transfers between devices, expert_output(): lax.all_to_all(partial_out.astype(jnp.bfloat16), 'expert', split_axis=0,...  160 us
    scatter x1, local copies, waits for them, and re-layouts, per_device(): buffer = buffer.at[target].set(normed[tok_index])  20.7 us
    gather x1, local copies, waits for them, and re-layouts, per_device(): picked = returned.reshape(experts_all * capacity, out_cols)[target]  11.9 us
    dot_general x1, matrix products, per_device(): jnp.einsum('sekd,edf->sekf', received, w_up, preferred_element_type=jnp.f...  10.1 us
    dot_general x1, matrix products, expert_output(): jnp.einsum('sekf,efd->sekd', hidden, w_down, preferred_element_type=jnp.f...  9.87 us
    dot_general x1, matrix products, per_device(): jnp.einsum('sekd,edf->sekf', received, w_gate, preferred_element_type=jnp...  8.58 us
  transfers between devices with their start and end apart: 1, of which 1 were waited for; matrix products, arithmetic and copies ran while one was open for 0% of the time, Pallas kernels for 0%

commit v1 on v0

--- a/solution.py
+++ b/solution.py
@@ -1,7 +1,302 @@
+import functools
+
 import jax
 import jax.numpy as jnp
 from jax import lax
+from jax.experimental import pallas as pl
+from jax.experimental.pallas import tpu as pltpu
 from jax.sharding import PartitionSpec as P
+
+UP_COLS = 256
+DOWN_COLS = 512
+LANES = 128
+
+
+def ring_place(index, n):
+    depth = n // 4
+    core, x, z = index % 2, (index // 2) % 2, index // 4
+    return 2 * (z + x * (2 * depth - 1 - 2 * z)) + core
+
+
+def ring_index(place, n):
+    depth = n // 4
+    core, q = place % 2, place // 2
+    x = q // depth
+    z = q + x * (2 * depth - 1 - 2 * q)
+    return (z * 2 + x) * 2 + core
+
+
+def left_slot(d):
+    return max(2 * d - 1, 0)
+
+
+def right_slot(d, n):
+    return n - 1 if d == n // 2 else 2 * d
+
+
+def return_order(n):
+    far = n // 2
+    order = [(far - 1, 1), (far, 0), (far - 1, 0)]
+    for d in range(far - 2, 0, -1):
+        order += [(d, 1), (d, 0)]
+    return order
+
+
+def groups_of(n):
+    far = n // 2
+    found = [(0, 3, 1)]
+    d = 2
+    while d < far - 2:
+        found.append((left_slot(d), 4, 2 * d + 1))
+        d += 2
+    while d < far:
+        found.append((left_slot(d), 2, 2 * d - 1))
+        d += 1
+    found.append((n - 1, 1, n - 2))
+    return found
+
+
+def ring_kernel(
+    n, attn, resid, gain, routes, codes, w_gate, w_up, w_down, out,
+    rows, parts, back, shares, scale, hidden, v_gate, v_up, v_down,
+    out_send, out_recv, share_send, share_recv, back_send, back_recv, load_sem,
+):
+    me = lax.axis_index("expert")
+    place = ring_place(me, n)
+    right = ring_index((place + 1) % n, n)
+    left = ring_index((place + n - 1) % n, n)
+    ways = ({"expert": right}, {"expert": left})
+    tok = resid.shape[0]
+    half = tok // 2
+    experts_pad = shares.shape[1]
+
+    barrier = pltpu.get_barrier_semaphore()
+    for way in ways:
+        pl.semaphore_signal(barrier, inc=1, device_id=way, device_id_type=pl.DeviceIdType.MESH)
+
+    loads = [
+        pltpu.make_async_copy(w_gate.at[0], v_gate, load_sem.at[0]),
+        pltpu.make_async_copy(w_up.at[0], v_up, load_sem.at[1]),
+        pltpu.make_async_copy(w_down.at[0], v_down, load_sem.at[2]),
+    ]
+    for load in loads:
+        load.start()
+
+    def norm(first, count):
+        at = pl.ds(first, count)
+        stream = resid[at, :].astype(jnp.float32) + attn[0, at, :].astype(jnp.float32)
+        mean_sq = jnp.mean(stream * stream, axis=1, keepdims=True)
+        scaled = stream * lax.rsqrt(mean_sq + 1e-06) * gain[...].astype(jnp.float32)
+        rows[at, :] = scaled.astype(jnp.bfloat16)
+
+    for first in range(0, tok, 16):
+        norm(first, 16)
+
+    code = codes[...].astype(jnp.float32)
+    weight = code / jnp.sum(code, axis=1, keepdims=True)
+    lane = lax.broadcasted_iota(jnp.int32, (tok, LANES), 1)
+    dense = jnp.zeros((tok, LANES), jnp.float32)
+    for k in range(routes.shape[1]):
+        dense = dense + jnp.where(lane == routes[:, k:k + 1], weight[:, k:k + 1], 0.0)
+    high = dense.astype(jnp.bfloat16).astype(jnp.float32)
+    both = jnp.concatenate([high, dense - high], axis=0)
+    shares[0] = both.T[:experts_pad].astype(jnp.bfloat16)
+
+    pl.semaphore_wait(barrier, 2)
+
+    def piece(slot, which):
+        return pl.ds(slot * tok + which * half, half)
+
+    def slot_of(way, d):
+        return left_slot(d) if way == 0 else right_slot(d, n)
+
+    def outward(way, j):
+        d, which = j // 2, (j % 2 if way == 0 else 1 - j % 2)
+        here, there = slot_of(way, d), slot_of(way, d + 1)
+        return pltpu.make_async_remote_copy(
+            rows.at[piece(here, which)], rows.at[piece(there, which)],
+            out_send.at[way, j], out_recv.at[way, j],
+            device_id=ways[way], device_id_type=pl.DeviceIdType.MESH,
+        )
+
+    def share(way, d):
+        return pltpu.make_async_remote_copy(
+            shares.at[slot_of(way, d)], shares.at[slot_of(way, d + 1)],
+            share_send.at[way, d], share_recv.at[way, d],
+            device_id=ways[way], device_id_type=pl.DeviceIdType.MESH,
+        )
+
+    def has_share(way, j):
+        return j % 2 == 0 and not (way == 1 and j // 2 == n // 2 - 1)
+
+    def send_out(way, j):
+        if has_share(way, j):
+            share(way, j // 2).start()
+        outward(way, j).start()
+
+    def arrive(j):
+        for way in range(2):
+            outward(way, j).wait_recv()
+            if has_share(way, j):
+                share(way, j // 2).wait_recv()
+            if j + 2 < n - 1:
+                send_out(way, j + 2)
+
+    for j in range(2):
+        for way in range(2):
+            send_out(way, j)
+
+    pick = (lax.broadcasted_iota(jnp.int32, (experts_pad, LANES), 0) == me).astype(jnp.bfloat16)
+
+    def prepare(first, count):
+        for slot in range(first, first + count):
+            wide = lax.dot_general(
+                shares[slot], pick, (((0,), (0,)), ((), ())), preferred_element_type=jnp.float32
+            )
+            scale[pl.ds(slot * tok, tok), :] = wide[:tok] + wide[tok:]
+
+    def up_step(first, count, c):
+        at = pl.ds(first * tok, count * tok)
+        cols = pl.ds(pl.multiple_of(c * UP_COLS, UP_COLS), UP_COLS)
+        x = rows[at, :]
+        gate = jnp.dot(x, v_gate[:, cols], preferred_element_type=jnp.float32)
+        up = jnp.dot(x, v_up[:, cols], preferred_element_type=jnp.float32)
+        factor = jnp.concatenate([scale[at, :]] * (UP_COLS // LANES), axis=1)
+        value = gate / (1.0 + jnp.exp(-gate)) * up * factor
+        hidden[pl.ds(0, count * tok), cols] = value.astype(jnp.bfloat16)
+
+    def down_step(first, count, c):
+        cols = pl.ds(pl.multiple_of(c * DOWN_COLS, DOWN_COLS), DOWN_COLS)
+        total = jnp.dot(
+            hidden[pl.ds(0, count * tok), :], v_down[:, cols], preferred_element_type=jnp.float32
+        )
+        parts[pl.ds(first * tok, count * tok), cols] = total.astype(jnp.bfloat16)
+
+    up_steps = v_gate.shape[1] // UP_COLS
+    down_steps = v_down.shape[1] // DOWN_COLS
+    up_cost = 2 * v_gate.shape[0] * UP_COLS
+    down_cost = v_down.shape[0] * DOWN_COLS
+    whole_cost = up_steps * up_cost + down_steps * down_cost
+
+    def multiply(first, count, begin, end):
+        def inside(done, cost):
+            return begin <= (done + cost / 2) / whole_cost < end
+
+        ups = [c for c in range(up_steps) if inside(c * up_cost, up_cost)]
+        downs = [c for c in range(down_steps) if inside(up_steps * up_cost + c * down_cost, down_cost)]
+        if ups:
+            @pl.loop(ups[0], ups[-1] + 1)
+            def _(c):
+                up_step(first, count, c)
+        if downs:
+            @pl.loop(downs[0], downs[-1] + 1)
+            def _(c):
+                down_step(first, count, c)
+
+    orders = return_order(n)
+
+    def backward(way, j):
+        d, which = orders[j]
+        which = which if way == 0 else 1 - which
+        slot = slot_of(1 - way, d)
+        return pltpu.make_async_remote_copy(
+            parts.at[piece(slot, which)], back.at[way, j],
+            back_send.at[way, j], back_recv.at[way, j],
+            device_id=ways[way], device_id_type=pl.DeviceIdType.MESH,
+        )
+
+    def send_back(way, j):
+        d, which = orders[j]
+        if (d + 1, which) in orders:
+            earlier = orders.index((d + 1, which))
+            backward(way, earlier).wait_recv()
+            at = piece(slot_of(1 - way, d), which if way == 0 else 1 - which)
+            total = parts[at, :].astype(jnp.float32) + back[way, earlier].astype(jnp.float32)
+            parts[at, :] = total.astype(jnp.bfloat16)
+        backward(way, j).start()
+
+    plan = groups_of(n)
+    arrived = -1
+    for g, (first, count, needed) in enumerate(plan):
+        while arrived < needed:
+            arrived += 1
+            arrive(arrived)
+        if g == 0:
+            for load in loads:
+                load.wait()
+        prepare(first, count)
+        later = plan[g + 1][2] if g + 1 < len(plan) else arrived
+        gaps = max(later - arrived, 1)
+        for gap in range(gaps):
+            multiply(first, count, gap / gaps, (gap + 1) / gaps if gap + 1 < gaps else 2.0)
+            if gap + 1 < gaps:
+                arrived += 1
+                arrive(arrived)
+        if g == len(plan) - 2:
+            for way in range(2):
+                send_back(way, 0)
+
+    for j in range(1, n - 1):
+        for way in range(2):
+            send_back(way, j)
+
+    for k in range(2):
+        which = 1 - k
+        at = pl.ds(which * half, half)
+        total = parts[at, :].astype(jnp.float32)
+        for way in range(2):
+            j = orders.index((1, which if way == 0 else 1 - which))
+            backward(way, j).wait_recv()
+            total = total + back[way, j].astype(jnp.float32)
+        out[at, :] = total.astype(jnp.bfloat16)
+
+    for way in range(2):
+        for j in range(n - 1):
+            outward(way, j).wait_send()
+            if has_share(way, j):
+                share(way, j // 2).wait_send()
+            backward(way, j).wait_send()
+
+
+def fused(n, attn_part, resid, norm_gain, routes, gate_codes, w_gate, w_up, w_down):
+    tok, width = resid.shape
+    ff = w_gate.shape[2]
+    vmem = pl.BlockSpec(memory_space=pltpu.VMEM)
+    hbm = pl.BlockSpec(memory_space=pltpu.HBM)
+    most = max(count for _, count, _ in groups_of(n))
+    dma = pltpu.SemaphoreType.DMA
+    return pl.pallas_call(
+        functools.partial(ring_kernel, n),
+        out_shape=jax.ShapeDtypeStruct((tok, width), jnp.bfloat16),
+        in_specs=[vmem] * 5 + [hbm] * 3,
+        out_specs=vmem,
+        scratch_shapes=[
+            pltpu.VMEM((n * tok, width), jnp.bfloat16),
+            pltpu.VMEM((n * tok, width), jnp.bfloat16),
+            pltpu.VMEM((2, n - 1, tok // 2, width), jnp.bfloat16),
+            pltpu.VMEM((n, -(-n // 16) * 16, LANES), jnp.bfloat16),
+            pltpu.VMEM((n * tok, LANES), jnp.float32),
+            pltpu.VMEM((most * tok, ff), jnp.bfloat16),
+            pltpu.VMEM((width, ff), jnp.bfloat16),
+            pltpu.VMEM((width, ff), jnp.bfloat16),
+            pltpu.VMEM((ff, width), jnp.bfloat16),
+            dma((2, n - 1)),
+            dma((2, n - 1)),
+            dma((2, n // 2)),
+            dma((2, n // 2)),
+            dma((2, n - 1)),
+            dma((2, n - 1)),
+            dma((3,)),
+        ],
+        compiler_params=pltpu.CompilerParams(
+            collective_id=0, has_side_effects=True, vmem_limit_bytes=60 * 1024 * 1024
+        ),
+        cost_estimate=pl.CostEstimate(
+            flops=6 * n * tok * width * ff,
+            bytes_accessed=6 * width * ff + 6 * tok * width,
+            transcendentals=n * tok * ff,
+        ),
+    )(attn_part, resid, norm_gain.reshape(1, width), routes, gate_codes, w_gate, w_up, w_down)
 
 
 def expert_output(hidden, w_down):
@@ -16,6 +311,12 @@
     top_count = routes.shape[1]
     n_expert = lax.axis_size("expert")
     local_experts = w_gate.shape[0]
+    fits = tok_count == 64 and local_experts == 1 and n_expert == 16
+    even = w_gate.shape[2] % UP_COLS == 0 and w_down.shape[2] % DOWN_COLS == 0
+    if lax.axis_size("tensor") == 1 and fits and even:
+        return fused(
+            n_expert, attn_part, resid, norm_gain, routes, gate_codes, w_gate, w_up, w_down
+        )
     experts_all = n_expert * local_experts
     capacity = min(tok_count, 3 * tok_count * top_count // experts_all)
     flat_routes = routes.reshape(-1)

time: 407 us -> 102 us (0.25)
  blocking collectives: 166 us -> 0 us
  waiting for transfers between devices: 160 us -> 0 us
  Pallas kernels: 0 us -> 94.6 us
  matrix products: 28.5 us -> 0 us
  local copies, waits for them, and re-layouts: 34.1 us -> 5.87 us
  other arithmetic: 11.3 us -> 0 us
  starting transfers between devices: 5.76 us -> 0 us
    all_to_all x1 -> x0, blocking collectives: 166 us -> none  [per_device(): lax.all_to_all(outgoing, 'expert', split_axis=0, concat_axis=0, tiled=True)]
    all_to_all x1 -> x0, waiting for transfers between devices: 160 us -> none  [expert_output(): lax.all_to_all(partial_out.astype(jnp.bfloat16), 'expert', split_axis=0,...]
    pallas_call x0 -> x1, Pallas kernels: none -> 94.6 us  [fused(): pl.pallas_call(functools.partial(ring_kernel, n), out_shape=jax.ShapeDtyp...]
    dot_general x3 -> x0, matrix products: 28.5 us -> none  [the longest x1 10.1 us: per_device(): jnp.einsum('sekd,edf->sekf', received, w_up, preferred_element_type=jnp.f...]
    scatter x1 -> x0, local copies, waits for them, and re-layouts: 20.7 us -> none  [per_device(): buffer = buffer.at[target].set(normed[tok_index])]
    gather x1 -> x0, local copies, waits for them, and re-layouts: 11.9 us -> none  [per_device(): picked = returned.reshape(experts_all * capacity, out_cols)[target]]
    reduce_sum x4 -> x0, other arithmetic: 7.34 us -> none  [the longest x1 5.82 us: per_device(): combined = jnp.sum(weighted.reshape(tok_count, top_count, out_cols), axis=1)]
    all_to_all x1 -> x0, starting transfers between devices: 5.76 us -> none  [expert_output(): lax.all_to_all(partial_out.astype(jnp.bfloat16), 'expert', split_axis=0,...]
  transfers between devices with their start and end apart: 1 -> 0, of which waited for: 1 -> 0; matrix products, arithmetic and copies ran while one was open for 0% -> 0% of each run, Pallas kernels for 0% -> 0%
where the time goes in v1:
time: 102 us; the launch traced here: 101 us
  Pallas kernels  94.6 us (93%)
  local copies, waits for them, and re-layouts  5.87 us (6%)
    pallas_call x1, Pallas kernels, fused(): pl.pallas_call(functools.partial(ring_kernel, n), out_shape=jax.ShapeDtyp...  94.6 us
    unnamed x3, local copies, waits for them, and re-layouts  4.57 us

profile of v1, /device:TPU:15, one launch (start us, length us, event | category | flops | bytes accessed | tf_op | source)
XLA Modules:
  0.0 100.5 jit_solution(17247563416392410242)
XLA Ops:
  0.0 1.3 %reshape.3.gain = bf16[1,3584]{1,0:T(2,128)(2,1)} reshape(bf16[3584]{0:T(1024)(128)(2,1)} %param.10) | data formatting | bytes 14336 | tf_op jit(solution)/shard_map/reshape | solution.py:299
  1.3 1.4 %copy.9.routes = s32[64,8]{1,0:T(8,128)} copy(s32[64,8]{0,1:T(8,128)} %param.11) | data formatting | bytes 4096 | tf_op args[3]
  2.7 1.4 %copy.10.codes = s32[64,8]{1,0:T(8,128)} copy(s32[64,8]{0,1:T(8,128)} %param.12) | data formatting | bytes 4096 | tf_op args[4]
  4.1 94.6 %shard_map.82 = bf16[64,3584]{1,0:T(8,128)(2,1)} custom-call(bf16[1,64,3584]{2,1,0:T(8,128)(2,1)} %attn.1, bf16[64,3584]{1,0:T(8,128)(2,1)} %resid.1, bf16[1,3584]{1,0:T(2,128)(2,1)} %reshape.3.gain, s32[64,8]{1,0:T(8,128)} %copy.9.routes, s32[64,8]{1,0:T(8,128)} %copy.10.codes, bf16[1,3584,1024]{2,1,0:T(8,128)(2,1)} %w_gate.1, bf16[1,3584,1024]{2,1,0:T(8,128)(2,1)} %w_up.1, ...), custom_call_target="tpu_custom_call" | custom-call | flops 22548578304 | bytes 23396352 | tf_op jit(solution)/shard_map/pallas_call | solution.py:268
  98.7 1.8 %copy.12 = bf16[64,3584]{1,0:T(8,128)(2,1)} copy(bf16[64,3584]{1,0:T(8,128)(2,1)} %shard_map.82) | data formatting | bytes 917504

commit v2 on v1

--- a/solution.py
+++ b/solution.py
@@ -36,23 +36,15 @@
 
 def return_order(n):
     far = n // 2
-    order = [(far - 1, 1), (far, 0), (far - 1, 0)]
+    order = [(far, 0), (far - 1, 1), (far - 1, 0)]
     for d in range(far - 2, 0, -1):
         order += [(d, 1), (d, 0)]
     return order
 
 
 def groups_of(n):
-    far = n // 2
-    found = [(0, 3, 1)]
-    d = 2
-    while d < far - 2:
-        found.append((left_slot(d), 4, 2 * d + 1))
-        d += 2
-    while d < far:
-        found.append((left_slot(d), 2, 2 * d - 1))
-        d += 1
-    found.append((n - 1, 1, n - 2))
+    found = [(left_slot(d), 4, 2 * d + 1) for d in range(1, n // 2 - 2, 2)]
+    found.append((n - 3, 3, n - 2))
     return found
 
 
@@ -86,21 +78,11 @@
         at = pl.ds(first, count)
         stream = resid[at, :].astype(jnp.float32) + attn[0, at, :].astype(jnp.float32)
         mean_sq = jnp.mean(stream * stream, axis=1, keepdims=True)
-        scaled = stream * lax.rsqrt(mean_sq + 1e-06) * gain[...].astype(jnp.float32)
+        scaled = stream * lax.rsqrt(mean_sq + 1e-06) * gain[...].astype(jnp.float32).reshape(1, -1)
         rows[at, :] = scaled.astype(jnp.bfloat16)
 
     for first in range(0, tok, 16):
         norm(first, 16)
-
-    code = codes[...].astype(jnp.float32)
-    weight = code / jnp.sum(code, axis=1, keepdims=True)
-    lane = lax.broadcasted_iota(jnp.int32, (tok, LANES), 1)
-    dense = jnp.zeros((tok, LANES), jnp.float32)
-    for k in range(routes.shape[1]):
-        dense = dense + jnp.where(lane == routes[:, k:k + 1], weight[:, k:k + 1], 0.0)
-    high = dense.astype(jnp.bfloat16).astype(jnp.float32)
-    both = jnp.concatenate([high, dense - high], axis=0)
-    shares[0] = both.T[:experts_pad].astype(jnp.bfloat16)
 
     pl.semaphore_wait(barrier, 2)
 
@@ -130,9 +112,9 @@
         return j % 2 == 0 and not (way == 1 and j // 2 == n // 2 - 1)
 
     def send_out(way, j):
-        if has_share(way, j):
+        outward(way, j).start()
+        if j > 0 and has_share(way, j):
             share(way, j // 2).start()
-        outward(way, j).start()
 
     def arrive(j):
         for way in range(2):
@@ -145,6 +127,18 @@
     for j in range(2):
         for way in range(2):
             send_out(way, j)
+
+    code = codes[...].astype(jnp.float32)
+    weight = code / jnp.sum(code, axis=0, keepdims=True)
+    expert = lax.broadcasted_iota(jnp.int32, (experts_pad, tok), 0)
+    dense = jnp.zeros((experts_pad, tok), jnp.float32)
+    for k in range(routes.shape[0]):
+        dense = dense + jnp.where(expert == routes[k:k + 1, :], weight[k:k + 1, :], 0.0)
+    high = dense.astype(jnp.bfloat16)
+    low = (dense - high.astype(jnp.float32)).astype(jnp.bfloat16)
+    shares[0] = jnp.concatenate([high, low], axis=1)
+    for way in range(2):
+        share(way, 0).start()
 
     pick = (lax.broadcasted_iota(jnp.int32, (experts_pad, LANES), 0) == me).astype(jnp.bfloat16)
 
@@ -232,13 +226,14 @@
             if gap + 1 < gaps:
                 arrived += 1
                 arrive(arrived)
-        if g == len(plan) - 2:
-            for way in range(2):
-                send_back(way, 0)
-
-    for j in range(1, n - 1):
+
+    prepare(0, 1)
+    spread = n - 5
+    for j in range(n - 1):
         for way in range(2):
             send_back(way, j)
+        if 1 <= j <= spread:
+            multiply(0, 1, (j - 1) / spread, j / spread if j < spread else 2.0)
 
     for k in range(2):
         which = 1 - k
@@ -296,7 +291,7 @@
             bytes_accessed=6 * width * ff + 6 * tok * width,
             transcendentals=n * tok * ff,
         ),
-    )(attn_part, resid, norm_gain.reshape(1, width), routes, gate_codes, w_gate, w_up, w_down)
+    )(attn_part, resid, norm_gain, routes.T, gate_codes.T, w_gate, w_up, w_down)
 
 
 def expert_output(hidden, w_down):

time: 102 us -> 96.2 us (0.943)
  local copies, waits for them, and re-layouts: 5.87 us -> 1.82 us
  Pallas kernels: 94.6 us -> 92.5 us
    unnamed x3 -> x1, local copies, waits for them, and re-layouts: 4.57 us -> 1.82 us
    pallas_call x1, Pallas kernels: 94.6 us -> 92.5 us  [fused(): pl.pallas_call(functools.partial(ring_kernel, n), out_shape=jax.ShapeDtyp...]
    reshape x1 -> x0, local copies, waits for them, and re-layouts: 1.3 us -> none  [fused(): norm_gain.reshape(1, width)]
where the time goes in v2:
time: 96.2 us; the launch traced here: 94.3 us
  Pallas kernels  92.5 us (96%)
  local copies, waits for them, and re-layouts  1.82 us (2%)
    pallas_call x1, Pallas kernels, fused(): pl.pallas_call(functools.partial(ring_kernel, n), out_shape=jax.ShapeDtyp...  92.5 us

profile of v2, /device:TPU:15, one launch (start us, length us, event | category | flops | bytes accessed | tf_op | source)
XLA Modules:
  0.0 94.3 jit_solution(4508393173203113898)
XLA Ops:
  0.0 92.5 %shard_map.82 = bf16[64,3584]{1,0:T(8,128)(2,1)} custom-call(bf16[1,64,3584]{2,1,0:T(8,128)(2,1)} %attn.1, bf16[64,3584]{1,0:T(8,128)(2,1)} %resid.1, bf16[3584]{0:T(1024)(128)(2,1)} %gain.1, s32[8,64]{1,0:T(8,128)} %bitcast.2, s32[8,64]{1,0:T(8,128)} %bitcast.3, bf16[1,3584,1024]{2,1,0:T(8,128)(2,1)} %w_gate.1, bf16[1,3584,1024]{2,1,0:T(8,128)(2,1)} %w_up.1, ...), custom_call_target="tpu_custom_call" | custom-call | flops 22548578304 | bytes 23396352 | tf_op jit(solution)/shard_map/pallas_call | solution.py:263
  92.5 1.8 %copy.10 = bf16[64,3584]{1,0:T(8,128)(2,1)} copy(bf16[64,3584]{1,0:T(8,128)(2,1)} %shard_map.82) | data formatting | bytes 917504
